TPU v7x, 512 devices: a whole 4x4x16 slice. The times are simulated.
512 devices in a mesh: section: 4 (over y), ctx: 32 (over x, z_lo), tp: 4 (over z_hi, core).
Axes of the slice: x: 4, y: 4, z: 16 (z_hi: 2, z_lo: 8; z = z_hi * 8 + z_lo), core: 2. Of those that a mesh axis runs over, the one named last changes fastest.
Arguments:
- queries: bfloat16 [4, 6144, 8192], P('section', 'ctx', 'tp'), may hold values from -180 to 180
- keys: bfloat16 [4, 6144, 1024], P('section', 'ctx', 'tp'), may hold values from -6 to 6
- values: bfloat16 [4, 6144, 1024], P('section', 'ctx', 'tp'), may hold values from -6 to 6
- modality: int32 [4, 6144], P('section', 'ctx'), may hold values from 0 to 1
- query_gain: float32 [2, 8192], P(None, 'tp'), may hold values from 0.5 to 1.5
- tower_key_gain: float32 [2, 1024], P(None, 'tp'), may hold values from 0.5 to 1.5
- doc_lengths: int32 [4, 16], P('section'), may hold values from 1 to 3840, 6144 in all within a row
Outputs:
- handed: bfloat16 [4, 6144, 8192], P('section', 'ctx', 'tp')
Inputs may be any that keep to these rules, and one draw needn't show every extreme that they name: `doc_lengths`: each row sums to 6144; its longest document has exactly 3840 tokens.
All inputs are finite; a program needn't handle non-finite values.
Results may differ from a plain program's by a relative error of at most 0.012.
The roundings to bfloat16 on the way count: a program that leaves them out, or rounds other values in their place, can miss the bound.
Values may be sent and summed in bfloat16 or wider, within the bound.
A program may use at most 64 MiB of HBM per device.

v0:
```python
import math

import jax
import jax.numpy as jnp
from jax import lax
from jax.sharding import PartitionSpec as P

HEAD_SIZE = 128


def passed_along(value, axis, steps):
    count = lax.axis_size(axis)
    pairs = [(source, (source + steps) % count) for source in range(count)]
    return lax.ppermute(value, axis, pairs)


def tower_scaled(inputs, towers, gains):
    chosen = jnp.where(towers[:, None] == 1, gains[1][None, :], gains[0][None, :])
    return (inputs.astype(jnp.float32) * chosen).astype(jnp.bfloat16)


def doc_index(bounds, places):
    return jnp.sum((places[:, None] >= bounds[None, :]).astype(jnp.int32), axis=1)


def body(queries, keys, values, modality, query_gain, tower_key_gain, doc_lengths):
    rows = queries.shape[1]
    width = queries.shape[2]
    kv_width = keys.shape[2]
    local_heads = width // HEAD_SIZE
    local_kv = kv_width // HEAD_SIZE
    query_group = local_heads // local_kv
    myself = lax.axis_index("ctx")
    query_row_slice = tower_scaled(queries[0], modality[0], query_gain)
    key_row_slice = tower_scaled(keys[0], modality[0], tower_key_gain)
    value_row_slice = values[0]
    bounds = jnp.cumsum(doc_lengths[0])[:-1]

    def place_of(owner, local):
        return owner * rows + local

    query_places = place_of(myself, jnp.arange(rows, dtype=jnp.int32))
    query_docs = doc_index(bounds, query_places)
    query_grid = query_row_slice.reshape(rows, local_kv, query_group, HEAD_SIZE)
    floor_value = -1e30
    start_state = (
        jnp.full((local_kv, query_group, rows), floor_value, jnp.float32),
        jnp.zeros((local_kv, query_group, rows), jnp.float32),
        jnp.zeros((local_kv, query_group, rows, HEAD_SIZE), jnp.float32),
    )
    carry = start_state
    key_piece = lax.all_gather(key_row_slice, "ctx", axis=0, tiled=True)
    value_piece = lax.all_gather(value_row_slice, "ctx", axis=0, tiled=True)
    block_count = key_piece.shape[0]
    current_block = math.gcd(block_count, 512)

    def one_block(state, offset):
        key_block = lax.dynamic_slice_in_dim(key_piece, offset, current_block, 0).reshape(
            current_block, local_kv, HEAD_SIZE
        )
        value_block = lax.dynamic_slice_in_dim(value_piece, offset, current_block, 0).reshape(
            current_block, local_kv, HEAD_SIZE
        )
        gathered = offset + jnp.arange(current_block, dtype=jnp.int32)
        key_places = place_of(gathered // rows, gathered % rows)
        key_docs = doc_index(bounds, key_places)
        visible = (key_places[None, :] <= query_places[:, None]) & (
            key_docs[None, :] == query_docs[:, None]
        )

        def update(current):
            peak, total, summed = current
            scores = jnp.einsum(
                "qkgd,tkd->kgqt", query_grid, key_block, preferred_element_type=jnp.float32
            ) * HEAD_SIZE ** (-0.5)
            scores = jnp.where(visible[None, None], scores, floor_value)
            new_peak = jnp.maximum(peak, jnp.max(scores, axis=-1))
            shrink = jnp.exp(peak - new_peak)
            weights = jnp.where(visible[None, None], jnp.exp(scores - new_peak[..., None]), 0.0)
            total = total * shrink + jnp.sum(weights, axis=-1)
            summed = summed * shrink[..., None] + jnp.einsum(
                "kgqt,tkd->kgqd",
                weights.astype(jnp.bfloat16),
                value_block,
                preferred_element_type=jnp.float32,
            )
            return (new_peak, total, summed)

        def keep(current):
            return current

        return (lax.cond(jnp.any(visible), update, keep, state), None)

    offsets = jnp.arange(block_count // current_block, dtype=jnp.int32) * current_block
    carry, unused = lax.scan(one_block, carry, offsets)
    running, total, summed = carry
    result = summed / total[..., None]
    result = jnp.transpose(result, (2, 0, 1, 3)).reshape(rows, width).astype(jnp.bfloat16)
    handed = passed_along(result, "section", 1)
    return handed[None]


def solution(mesh):
    placed = (
        P("section", "ctx", "tp"),
        P("section", "ctx", "tp"),
        P("section", "ctx", "tp"),
        P("section", "ctx"),
        P(None, "tp"),
        P(None, "tp"),
        P("section", None),
    )
    return jax.shard_map(
        body, mesh=mesh, in_specs=placed, out_specs=P("section", "ctx", "tp"), check_vma=False
    )
```

profile of v0, /device:TPU:174, one launch (start us, length us, event | category | flops | bytes accessed | tf_op | source)
XLA Modules:
  0.0 612.2 jit_solution(17002929581125979272)
XLA Ops:
  13.5 222.1 %all-gather.6.cloned.1.call-done = bf16[1,6144,256]{2,1,0:T(8,128)(2,1)} async-done(((bf16[1,192,256]{2,1,0:T(8,128)(2,1)}), bf16[1,6144,256]{2,1,0:T(8,128)(2,1)}) %all-gather.6.cloned.1.call-update) | async-done | bytes 3145744 | tf_op jit(solution)/shard_map/all_gather | solution.py:53
  235.6 4.7 copy.29
  240.3 228.3 %all-gather.4.cloned.1.call-done = bf16[6144,256]{1,0:T(8,128)(2,1)} async-done(((bf16[192,256]{1,0:T(8,128)(2,1)}), bf16[6144,256]{1,0:T(8,128)(2,1)}) %all-gather.4.cloned.1.call-update) | async-done | bytes 3145744 | tf_op jit(solution)/shard_map/all_gather | solution.py:52
  468.6 4.7 copy.27
  473.5 115.8 %while.17 = (s32[]{:T(128)}, f32[2,8,192]{2,1,0:T(8,128)S(1)}, f32[2,8,192]{2,1,0:T(8,128)S(1)}, f32[2,8,192,128]{3,2,1,0:T(8,128)S(1)}, s32[12]{0:T(128)S(1)}, ...) while((s32[]{:T(128)}, f32[2,8,192]{2,1,0:T(8,128)S(1)}, ...), condition=%wide.region_9.10_spmd.clone, body=%wide.region_2.9_spmd.clone.sunk | while | flops 826969792 | bytes 24982128 | solution.py:95
  484.5 9.2 %conditional.3 = ((f32[2,8,192]{2,1,0:T(8,128)S(1)}, f32[2,8,192]{2,1,0:T(8,128)S(1)}, f32[2,8,192,128]{3,2,1,0:T(8,128)S(1)})) conditional(s32[]{:T(128)} %convert_element_type.79, (f32[2,8,192]{2,1,0:T(8,128)S(1)}, f32[2,8,192]{2,1,0:T(8,128)S(1)}, f32[2,8,192,128]{3,2,1,0:T(8,128)S(1)}) %tuple.60, (pred[192,512]{1,0:T(8,128)(4,1)S(1)}, s32[]{:T(128)}, ...), branch_computations={%region_5.5_spmd, %region_6.8_spmd} | conditional | flops 826546176 | bytes 24870982 | solution.py:92
  491.3 2.5 multiply_add_fusion
  496.5 9.2 %conditional.3 = ((f32[2,8,192]{2,1,0:T(8,128)S(1)}, f32[2,8,192]{2,1,0:T(8,128)S(1)}, f32[2,8,192,128]{3,2,1,0:T(8,128)S(1)})) conditional(s32[]{:T(128)} %convert_element_type.79, (f32[2,8,192]{2,1,0:T(8,128)S(1)}, f32[2,8,192]{2,1,0:T(8,128)S(1)}, f32[2,8,192,128]{3,2,1,0:T(8,128)S(1)}) %tuple.60, (pred[192,512]{1,0:T(8,128)(4,1)S(1)}, s32[]{:T(128)}, ...), branch_computations={%region_5.5_spmd, %region_6.8_spmd} | conditional | flops 826546176 | bytes 24870982 | solution.py:92
  503.2 2.5 multiply_add_fusion
  508.4 9.2 %conditional.3 = ((f32[2,8,192]{2,1,0:T(8,128)S(1)}, f32[2,8,192]{2,1,0:T(8,128)S(1)}, f32[2,8,192,128]{3,2,1,0:T(8,128)S(1)})) conditional(s32[]{:T(128)} %convert_element_type.79, (f32[2,8,192]{2,1,0:T(8,128)S(1)}, f32[2,8,192]{2,1,0:T(8,128)S(1)}, f32[2,8,192,128]{3,2,1,0:T(8,128)S(1)}) %tuple.60, (pred[192,512]{1,0:T(8,128)(4,1)S(1)}, s32[]{:T(128)}, ...), branch_computations={%region_5.5_spmd, %region_6.8_spmd} | conditional | flops 826546176 | bytes 24870982 | solution.py:92
  515.2 2.5 multiply_add_fusion
  520.4 9.2 %conditional.3 = ((f32[2,8,192]{2,1,0:T(8,128)S(1)}, f32[2,8,192]{2,1,0:T(8,128)S(1)}, f32[2,8,192,128]{3,2,1,0:T(8,128)S(1)})) conditional(s32[]{:T(128)} %convert_element_type.79, (f32[2,8,192]{2,1,0:T(8,128)S(1)}, f32[2,8,192]{2,1,0:T(8,128)S(1)}, f32[2,8,192,128]{3,2,1,0:T(8,128)S(1)}) %tuple.60, (pred[192,512]{1,0:T(8,128)(4,1)S(1)}, s32[]{:T(128)}, ...), branch_computations={%region_5.5_spmd, %region_6.8_spmd} | conditional | flops 826546176 | bytes 24870982 | solution.py:92
  527.1 2.5 multiply_add_fusion
  532.4 9.2 %conditional.3 = ((f32[2,8,192]{2,1,0:T(8,128)S(1)}, f32[2,8,192]{2,1,0:T(8,128)S(1)}, f32[2,8,192,128]{3,2,1,0:T(8,128)S(1)})) conditional(s32[]{:T(128)} %convert_element_type.79, (f32[2,8,192]{2,1,0:T(8,128)S(1)}, f32[2,8,192]{2,1,0:T(8,128)S(1)}, f32[2,8,192,128]{3,2,1,0:T(8,128)S(1)}) %tuple.60, (pred[192,512]{1,0:T(8,128)(4,1)S(1)}, s32[]{:T(128)}, ...), branch_computations={%region_5.5_spmd, %region_6.8_spmd} | conditional | flops 826546176 | bytes 24870982 | solution.py:92
  539.1 2.5 multiply_add_fusion
  544.3 9.2 %conditional.3 = ((f32[2,8,192]{2,1,0:T(8,128)S(1)}, f32[2,8,192]{2,1,0:T(8,128)S(1)}, f32[2,8,192,128]{3,2,1,0:T(8,128)S(1)})) conditional(s32[]{:T(128)} %convert_element_type.79, (f32[2,8,192]{2,1,0:T(8,128)S(1)}, f32[2,8,192]{2,1,0:T(8,128)S(1)}, f32[2,8,192,128]{3,2,1,0:T(8,128)S(1)}) %tuple.60, (pred[192,512]{1,0:T(8,128)(4,1)S(1)}, s32[]{:T(128)}, ...), branch_computations={%region_5.5_spmd, %region_6.8_spmd} | conditional | flops 826546176 | bytes 24870982 | solution.py:92
  551.1 2.5 multiply_add_fusion
  556.3 9.2 %conditional.3 = ((f32[2,8,192]{2,1,0:T(8,128)S(1)}, f32[2,8,192]{2,1,0:T(8,128)S(1)}, f32[2,8,192,128]{3,2,1,0:T(8,128)S(1)})) conditional(s32[]{:T(128)} %convert_element_type.79, (f32[2,8,192]{2,1,0:T(8,128)S(1)}, f32[2,8,192]{2,1,0:T(8,128)S(1)}, f32[2,8,192,128]{3,2,1,0:T(8,128)S(1)}) %tuple.60, (pred[192,512]{1,0:T(8,128)(4,1)S(1)}, s32[]{:T(128)}, ...), branch_computations={%region_5.5_spmd, %region_6.8_spmd} | conditional | flops 826546176 | bytes 24870982 | solution.py:92
  563.0 2.5 multiply_add_fusion
  568.2 9.2 %conditional.3 = ((f32[2,8,192]{2,1,0:T(8,128)S(1)}, f32[2,8,192]{2,1,0:T(8,128)S(1)}, f32[2,8,192,128]{3,2,1,0:T(8,128)S(1)})) conditional(s32[]{:T(128)} %convert_element_type.79, (f32[2,8,192]{2,1,0:T(8,128)S(1)}, f32[2,8,192]{2,1,0:T(8,128)S(1)}, f32[2,8,192,128]{3,2,1,0:T(8,128)S(1)}) %tuple.60, (pred[192,512]{1,0:T(8,128)(4,1)S(1)}, s32[]{:T(128)}, ...), branch_computations={%region_5.5_spmd, %region_6.8_spmd} | conditional | flops 826546176 | bytes 24870982 | solution.py:92
  575.0 2.5 multiply_add_fusion
  580.2 9.2 %conditional.3 = ((f32[2,8,192]{2,1,0:T(8,128)S(1)}, f32[2,8,192]{2,1,0:T(8,128)S(1)}, f32[2,8,192,128]{3,2,1,0:T(8,128)S(1)})) conditional(s32[]{:T(128)} %convert_element_type.79, (f32[2,8,192]{2,1,0:T(8,128)S(1)}, f32[2,8,192]{2,1,0:T(8,128)S(1)}, f32[2,8,192,128]{3,2,1,0:T(8,128)S(1)}) %tuple.60, (pred[192,512]{1,0:T(8,128)(4,1)S(1)}, s32[]{:T(128)}, ...), branch_computations={%region_5.5_spmd, %region_6.8_spmd} | conditional | flops 826546176 | bytes 24870982 | solution.py:92
  586.9 2.5 multiply_add_fusion
  592.5 12.0 %collective-permute-done = bf16[192,2048]{1,0:T(8,128)(2,1)S(1)} collective-permute-done((bf16[192,2048]{1,0:T(8,128)(2,1)S(1)}, bf16[192,2048]{1,0:T(8,128)(2,1)S(1)}, u32[]{:S(2)}, u32[]{:S(2)}) %collective-permute-start) | collective-permute-done | bytes 786464 | tf_op jit(solution)/shard_map/ppermute | solution.py:14
  (145 shorter events, 79.5 us)
Async XLA Ops:
  6.5 6.2 %copy-start = (f32[2,2048]{1,0:T(2,128)S(1)}, f32[2,2048]{1,0:T(2,128)}, u32[]{:S(2)}) copy-start(f32[2,2048]{1,0:T(2,128)} %param.15) | copy-start | bytes 49156
  6.5 229.1 %all-gather.6.cloned.1.call-start = ((), (), s32[]{:S(2)}) async-start(), calls=%async_computation.1 | async-start | bytes 3244032 | tf_op jit(solution)/shard_map/all_gather | solution.py:53
  7.3 461.4 %all-gather.4.cloned.1.call-start = ((), (), s32[]{:S(2)}) async-start(), calls=%async_computation | async-start | bytes 3244032 | tf_op jit(solution)/shard_map/all_gather | solution.py:52
  590.6 13.9 %collective-permute-start = (bf16[192,2048]{1,0:T(8,128)(2,1)S(1)}, bf16[192,2048]{1,0:T(8,128)(2,1)S(1)}, u32[]{:S(2)}, u32[]{:S(2)}) collective-permute-start(bf16[192,2048]{1,0:T(8,128)(2,1)S(1)} %bitcast.56), channel_id=1, source_target_pairs={{0,128},{128,256},{256,384},{384,0},{1,129},{129,257},{257,385},{3... | collective-permute-start | bytes 2359304 | tf_op jit(solution)/shard_map/ppermute | solution.py:14
Sparse Core Ops, SparseCore 0:
  9.4 226.1 all-gather.5
  237.7 230.8 all-gather.3
where the time goes:
time: 612 us
  waiting for transfers between devices  463 us (76%)
  other arithmetic  42.1 us (7%)
  matrix products  33.8 us (6%)
  local copies, waits for them, and re-layouts  32.4 us (5%)
  loops' own time  25.3 us (4%)
  between operations  13.5 us (2%)
    all_gather x1, waiting for transfers between devices, body(): key_piece = lax.all_gather(key_row_slice, 'ctx', axis=0, tiled=True)  228 us
    all_gather x1, waiting for transfers between devices, body(): value_piece = lax.all_gather(value_row_slice, 'ctx', axis=0, tiled=True)  222 us
    dot_general x9, matrix products, update(): jnp.einsum('kgqt,tkd->kgqd', weights.astype(jnp.bfloat16), value_block, p...  22.1 us
    reduce_sum x9, other arithmetic, update(): total = total * shrink + jnp.sum(weights, axis=-1)  18.8 us
    another operation x12, loops' own time, one_block(): return (lax.cond(jnp.any(visible), update, keep, state), None)  18 us
  transfers between devices with their start and end apart: 3, of which 3 were waited for; matrix products, arithmetic and copies ran while one was open for 2% of the time, Pallas kernels for 0%

commit v1 on v0

v1 whole, which is shorter than its diff:
```python
import functools

import jax
import jax.numpy as jnp
from jax import lax
from jax.experimental import pallas as pl
from jax.experimental.pallas import tpu as pltpu
from jax.sharding import PartitionSpec as P

MESH = pl.DeviceIdType.MESH
NT = (((1,), (1,)), ((), ()))
HEAD = 128
ROWS = 192
KV_HEADS = 2
GROUP = 8
HEADS = KV_HEADS * GROUP
BLOCKS = 32
WINDOW = 20
SLOTS = 32
OWN = 31
PER_GROUP = 4
GROUP_KEYS = PER_GROUP * ROWS
KEY_GROUPS = WINDOW // PER_GROUP
BIG = float(1 << 20)
LOG2E = 1.4426950408889634
EXP_SCALE = HEAD ** -0.5 * LOG2E
DIAGONAL = 7

SCHEDULE = (
    (
        0, 64, 129, 193, 258, 322, 387, 451, 516, 580, 612, 645, 677, 709, 774, 838, 870, 903, 935, 1032,
        1096, 1161, 1225, 1290, 1354, 1419, 1483, 1548, 1612, 1677, 1741, 1806, 1870, 1935, 2064, 2128,
        2193, 2257, 2322, 2386, 2451, 2515, 2580, 2644, 2709, 2773, 2838, 2902, 2967, 3160, 3289, 3418,
        3547, 3676, 3805, 3934,
    ),
    (
        128, 192, 257, 321, 386, 450, 484, 515, 579, 646, 678, 708, 773, 837, 902, 1024, 1160, 1224, 1249,
        1289, 1353, 1378, 1418, 1482, 1507, 1540, 1611, 1636, 1669, 1740, 1765, 1798, 1869, 1927, 2023,
        2056, 2192, 2256, 2281, 2314, 2385, 2410, 2443, 2514, 2539, 2572, 2643, 2668, 2708, 2765, 2797,
        2837, 2894, 2926, 2966, 3055, 3288, 3313, 3417, 3442, 3546, 3571, 3675, 3700, 3804, 3829, 3933,
        3958, 4087,
    ),
    (
        256, 320, 356, 385, 449, 514, 578, 643, 707, 772, 836, 901, 1025, 1152, 1250, 1288, 1352, 1379,
        1417, 1481, 1508, 1546, 1610, 1637, 1670, 1707, 1739, 1766, 1804, 1868, 1895, 1933, 2057, 2186,
        2282, 2315, 2384, 2411, 2444, 2513, 2540, 2578, 2642, 2669, 2707, 2771, 2798, 2831, 2901, 2927,
        2958, 3047, 3144, 3280, 3314, 3416, 3443, 3545, 3572, 3674, 3701, 3796, 3830, 3925, 3959, 4071,
    ),
    (
        132, 228, 384, 448, 513, 577, 642, 683, 706, 771, 835, 900, 1026, 1155, 1251, 1280, 1413, 1480,
        1509, 1542, 1609, 1638, 1671, 1738, 1767, 1803, 1867, 1892, 1932, 2058, 2113, 2187, 2283, 2316,
        2376, 2412, 2441, 2512, 2541, 2570, 2641, 2670, 2706, 2770, 2799, 2835, 2899, 2924, 2959, 3145,
        3272, 3315, 3410, 3444, 3544, 3573, 3673, 3702, 3803, 3831, 3892, 3924, 3951, 4078,
    ),
    (
        4, 36, 512, 576, 641, 705, 770, 834, 899, 1027, 1156, 1285, 1381, 1414, 1510, 1543, 1608, 1639,
        1673, 1737, 1802, 1866, 1931, 2059, 2114, 2188, 2243, 2284, 2317, 2368, 2413, 2446, 2504, 2542,
        2576, 2640, 2671, 2705, 2769, 2789, 2834, 2898, 2923, 2956, 3281, 3316, 3408, 3445, 3531, 3574,
        3672, 3703, 3801, 3823, 3932, 3950, 4020,
    ),
    (
        640, 704, 769, 833, 898, 1028, 1157, 1253, 1286, 1382, 1415, 1511, 1538, 1672, 1736, 1801, 1865,
        1925, 2060, 2189, 2242, 2285, 2313, 2371, 2414, 2449, 2496, 2543, 2574, 2628, 2660, 2704, 2768,
        2793, 2828, 2897, 2922, 2955, 3317, 3400, 3446, 3529, 3575, 3627, 3658, 3695, 3800, 3827, 3929,
    ),
    (
        768, 832, 897, 1029, 1158, 1254, 1287, 1383, 1409, 1537, 1667, 1800, 1864, 1930, 2061, 2190, 2244,
        2286, 2310, 2370, 2415, 2439, 2499, 2573, 2626, 2697, 2757, 2829, 2896, 2961, 3318, 3402, 3447,
        3528, 3566, 3660, 3802, 3825, 3922, 4075,
    ),
    (
        896, 1030, 1159, 1255, 1281, 1665, 1794, 1924, 2053, 2182, 2287, 2311, 2445, 2701, 2756, 2832,
        2888, 2960, 3310, 3567, 3793, 3931,
    ),
    (
        1031, 1795, 1923, 2054, 2183, 2826, 2889, 2963, 3141, 3319, 3439, 3930,
    ),
    (
        1926, 2055, 2957, 3311, 3928,
    ),
)
ROUNDS = len(SCHEDULE)


def neighbour(chip, direction):
    x, z = divmod(chip, 8)
    return (
        ((x + 1) % 4) * 8 + z,
        ((x + 3) % 4) * 8 + z,
        chip + 1,
        chip - 1,
    )[direction]


def relay_tables():
    slot = [{chip: OWN} for chip in range(BLOCKS)]
    count = [0] * BLOCKS
    spare = [WINDOW] * BLOCKS
    sends = [[[1023] * ROUNDS for _ in range(4)] for _ in range(BLOCKS)]
    takes = [[[31] * ROUNDS for _ in range(4)] for _ in range(BLOCKS)]
    ready = [[0] * ROUNDS for _ in range(BLOCKS)]
    for step, entries in enumerate(SCHEDULE):
        known = [dict(held) for held in slot]
        for entry in entries:
            link, block = divmod(entry, 32)
            sender, direction = divmod(link, 4)
            target = neighbour(sender, direction)
            if max(0, target - WINDOW) <= block < target:
                place = count[target]
                count[target] += 1
            else:
                place = spare[target]
                spare[target] += 1
            assert place < OWN and block not in slot[target]
            slot[target][block] = place
            sends[sender][direction][step] = known[sender][block] * 32 + place
            takes[target][direction][step] = place
        for chip in range(BLOCKS):
            ready[chip][step] = count[chip] // PER_GROUP
    for chip in range(BLOCKS):
        assert count[chip] == min(chip, WINDOW)
        ready[chip][ROUNDS - 1] = -(-count[chip] // PER_GROUP)
    owners = [[31] * WINDOW for _ in range(BLOCKS)]
    for chip in range(BLOCKS):
        for block, place in slot[chip].items():
            if place < WINDOW:
                owners[chip][place] = block
    return sends, takes, ready, owners, count


def packed(values, bits):
    per = 30 // bits
    return [
        sum(value << (bits * i) for i, value in enumerate(values[at : at + per]))
        for at in range(0, len(values), per)
    ]


def chosen(chip, per_chip):
    result = jnp.int32(per_chip[0])
    for index in range(1, len(per_chip)):
        if per_chip[index] != per_chip[0]:
            result = jnp.where(chip == index, jnp.int32(per_chip[index]), result)
    return result


class Table:
    def __init__(self, chip, per_chip, bits):
        self.bits = bits
        self.per = 30 // bits
        rows = [packed(values, bits) for values in per_chip]
        self.words = [chosen(chip, column) for column in zip(*rows)]

    def at(self, index):
        word = self.words[0]
        for place in range(1, len(self.words)):
            word = jnp.where(index >= place * self.per, self.words[place], word)
        shift = lax.rem(index, self.per) * self.bits
        return lax.shift_right_logical(word, shift) & ((1 << self.bits) - 1)


ITEMS = ((0, 7), (0, 0), (0, 1), (1, 7), (1, 0), (1, 1), (0, 2), (1, 2), (0, 3), (1, 3), (0, 4), (1, 4))
HALVES = 2
UNITS = len(ITEMS) * HALVES
FIRST_STEP = 12
SECOND_STEP = 21
COMM_STEPS = ROUNDS * 4
STEPS = COMM_STEPS + UNITS
QUERY_COPIES = 8


def one_hot_rows(places, first, last):
    inside = (places >= first) & (places < last)
    return inside


def kernel(
    q_ref, k_ref, v_ref, modality_ref, q_gain_ref, k_gain_ref, docs_ref, o_ref,
    kv, key_stage, query_stage, queries, docs_stage, docs_in, key_docs, query_docs,
    peak, total, summed,
    link_send, link_recv, hop_send, hop_recv, query_send, query_recv, docs_sems,
):
    section = lax.axis_index("section")
    chip = lax.axis_index("ctx")
    part = lax.axis_index("tp")
    x, z = chip // 8, lax.rem(chip, 8)
    after = (lax.rem(section + 1, 4), chip, part)
    before = (lax.rem(section + 3, 4), chip, part)
    around = (
        (section, lax.rem(x + 1, 4) * 8 + z, part),
        (section, lax.rem(x + 3, 4) * 8 + z, part),
        (section, x * 8 + jnp.minimum(z + 1, 7), part),
        (section, x * 8 + jnp.maximum(z - 1, 0), part),
    )
    exists = (None, None, z < 7, z > 0)

    barrier = pltpu.get_barrier_semaphore()
    for device in (after, before, around[0], around[1]):
        pl.semaphore_signal(barrier, inc=1, device_id=device, device_id_type=MESH)
    for direction in (2, 3):
        @pl.when(exists[direction])
        def _():
            pl.semaphore_signal(barrier, inc=1, device_id=around[direction], device_id_type=MESH)
    pl.semaphore_wait(barrier, 4 + (z < 7).astype(jnp.int32) + (z > 0).astype(jnp.int32))

    diagonal = lax.broadcasted_iota(jnp.int32, (ROWS, ROWS), 0) == lax.broadcasted_iota(
        jnp.int32, (ROWS, ROWS), 1
    )
    towers = jnp.sum(
        jnp.where(diagonal, modality_ref[0:1, :].astype(jnp.float32), 0.0), axis=1, keepdims=True
    )
    image = jnp.broadcast_to(towers, (ROWS, HEAD)) > 0.5

    def scaled(values, gain_ref, channels):
        gains = jnp.where(image, gain_ref[1:2, channels], gain_ref[0:1, channels])
        return (values.astype(jnp.float32) * gains).astype(jnp.bfloat16)

    def hop(stream):
        head, kind = stream // 2, stream % 2
        if kind == 0:
            source = key_stage.at[head]
        else:
            source = v_ref.at[0, :, pl.ds(head * HEAD, HEAD)]
        return pltpu.make_async_remote_copy(
            src_ref=source, dst_ref=kv.at[head, OWN, kind],
            send_sem=hop_send.at[stream], recv_sem=hop_recv.at[stream],
            device_id=after, device_id_type=MESH,
        )

    for head in range(KV_HEADS):
        channels = pl.ds(head * HEAD, HEAD)
        key_stage[head] = scaled(k_ref[0, :, channels], k_gain_ref, channels)
        hop(2 * head).start()
        hop(2 * head + 1).start()

    docs_stage[...] = jnp.zeros_like(docs_stage)
    docs_stage[0:1, 0:16] = docs_ref[...]
    docs_copy = pltpu.make_async_remote_copy(
        src_ref=docs_stage, dst_ref=docs_in, send_sem=docs_sems.at[0], recv_sem=docs_sems.at[1],
        device_id=after, device_id_type=MESH,
    )
    docs_copy.start()

    sends, takes, ready, owners, count = relay_tables()
    send_tables = [Table(chip, [sends[c][d] for c in range(BLOCKS)], 10) for d in range(4)]
    take_tables = [Table(chip, [takes[c][d] for c in range(BLOCKS)], 5) for d in range(4)]
    ready_table = Table(chip, ready, 3)
    owner_table = Table(chip, owners, 5)
    arrivals = jnp.minimum(chip, WINDOW)
    groups = (arrivals + PER_GROUP - 1) // PER_GROUP

    def link_copy(direction, step, stream, source, target):
        head, kind = stream // 2, lax.rem(stream, 2)
        return pltpu.make_async_remote_copy(
            src_ref=kv.at[head, source, kind], dst_ref=kv.at[head, target, kind],
            send_sem=link_send.at[direction, step, stream],
            recv_sem=link_recv.at[direction, step, stream],
            device_id=around[direction], device_id_type=MESH,
        )

    def start_round(step, stream):
        for direction in range(4):
            code = send_tables[direction].at(step)

            @pl.when(code != 1023)
            def _():
                link_copy(direction, step, stream, code // 32, lax.rem(code, 32)).start()

    def take_round(step, stream):
        for direction in range(4):
            place = take_tables[direction].at(step)

            @pl.when(place != 31)
            def _():
                link_copy(direction, step, stream, place, place).wait_recv()

    def query_copy(index):
        heads = pl.ds(index * (HEADS // QUERY_COPIES), HEADS // QUERY_COPIES)
        return pltpu.make_async_remote_copy(
            src_ref=query_stage.at[heads], dst_ref=queries.at[heads],
            send_sem=query_send.at[index], recv_sem=query_recv.at[index],
            device_id=after, device_id_type=MESH,
        )

    for head in range(HEADS):
        channels = pl.ds(head * HEAD, HEAD)
        query_stage[head] = scaled(q_ref[0, :, channels], q_gain_ref, channels)

    for stream in range(4):
        hop(stream).wait_recv()
        start_round(jnp.int32(0), jnp.int32(stream))
    for index in range(QUERY_COPIES):
        query_copy(index).start()

    def clear(place, carry):
        for head in range(KV_HEADS):
            kv[head, place] = jnp.zeros((2, ROWS, HEAD), jnp.bfloat16)
        return carry

    lax.fori_loop(arrivals, groups * PER_GROUP, clear, 0)

    docs_copy.wait_recv()
    lengths = docs_in[0:1, :].astype(jnp.float32)
    square = (HEAD, HEAD)
    down = lax.broadcasted_iota(jnp.int32, square, 0)
    across = lax.broadcasted_iota(jnp.int32, square, 1)
    column = jnp.sum(jnp.where(down == across, lengths, 0.0), axis=1, keepdims=True)
    first = jnp.sum(jnp.where(down < across, column, 0.0), axis=0, keepdims=True)
    lane = lax.broadcasted_iota(jnp.int32, (1, HEAD), 1)
    last = jnp.where(lane == 15, 1e9, first + lengths)
    first = jnp.where(lane < 16, first, jnp.where(lane == 16, -1e9, 1e9))
    last = jnp.where(lane < 16, last, jnp.where(lane == 16, 0.0, 1e9))
    inner = lax.broadcasted_iota(jnp.int32, (ROWS, HEAD), 0)

    def members(block):
        places = (inner + block * ROWS).astype(jnp.float32)
        return (places >= first) & (places < last)

    def mark(place, carry):
        block = jnp.where(place < arrivals, owner_table.at(place), -1)
        key_docs[place] = jnp.where(members(block), 1.0, 0.0).astype(jnp.bfloat16)
        return carry

    lax.fori_loop(0, groups * PER_GROUP, mark, 0)
    own_members = members(chip)
    key_docs[WINDOW] = jnp.where(own_members, 1.0, 0.0).astype(jnp.bfloat16)
    query_docs[...] = jnp.where(own_members, 0.0, -BIG).astype(jnp.bfloat16)

    heads_per_unit = GROUP // HALVES
    causal = lax.broadcasted_iota(jnp.int32, (ROWS, ROWS), 1) <= lax.broadcasted_iota(
        jnp.int32, (ROWS, ROWS), 0
    )

    def attend_own(head, half):
        keys = jnp.concatenate([kv[head, OWN, 0], key_docs[WINDOW]], axis=1)
        values = jnp.concatenate([kv[head, OWN, 1], jnp.ones((ROWS, HEAD), jnp.bfloat16)], axis=1)
        marks = query_docs[...]
        for index in range(heads_per_unit):
            row = head * GROUP + half * heads_per_unit + index
            rows = jnp.concatenate([queries[row], marks], axis=1)
            scores = lax.dot_general(rows, keys, NT, preferred_element_type=jnp.float32)
            scores = jnp.where(causal, scores, -1e30)
            top = jnp.max(scores, axis=1, keepdims=True)
            weights = jnp.exp2((scores - top) * EXP_SCALE).astype(jnp.bfloat16)
            mixed = jnp.dot(weights, values, preferred_element_type=jnp.float32)
            peak[row] = jnp.broadcast_to(top, (ROWS, HEAD))
            summed[row] = mixed[:, :HEAD]
            total[row] = mixed[:, HEAD:]

    def attend_group(head, group, half):
        slots = pl.ds(group * PER_GROUP, PER_GROUP)
        keys = jnp.concatenate(
            [kv[head, slots, 0].reshape(GROUP_KEYS, HEAD), key_docs[slots].reshape(GROUP_KEYS, HEAD)],
            axis=1,
        )
        values = jnp.concatenate(
            [kv[head, slots, 1].reshape(GROUP_KEYS, HEAD), jnp.ones((GROUP_KEYS, HEAD), jnp.bfloat16)],
            axis=1,
        )
        marks = query_docs[...]
        for index in range(heads_per_unit):
            row = head * GROUP + half * heads_per_unit + index
            rows = jnp.concatenate([queries[row], marks], axis=1)
            scores = lax.dot_general(rows, keys, NT, preferred_element_type=jnp.float32)
            old = peak[row]
            new = jnp.maximum(old, jnp.max(scores, axis=1, keepdims=True))
            shrink = jnp.exp2((old - new) * EXP_SCALE)
            weights = jnp.exp2((scores - new[:, 0:1]) * EXP_SCALE).astype(jnp.bfloat16)
            mixed = jnp.dot(weights, values, preferred_element_type=jnp.float32)
            peak[row] = new
            summed[row] = summed[row] * shrink + mixed[:, :HEAD]
            total[row] = total[row] * shrink + mixed[:, HEAD:]

    item_words = packed([head * 8 + group for head, group in ITEMS], 4)

    def step_body(index, done):
        step, stream = index // 4, lax.rem(index, 4)
        at = jnp.minimum(step, ROUNDS - 1)

        @pl.when(step < ROUNDS)
        def _():
            take_round(step, stream)

            @pl.when(step + 1 < ROUNDS)
            def _():
                start_round(step + 1, stream)

        @pl.when(index == FIRST_STEP)
        def _():
            for copy in range(QUERY_COPIES // 2):
                query_copy(copy).wait_recv()

        @pl.when(index == SECOND_STEP)
        def _():
            for copy in range(QUERY_COPIES // 2, QUERY_COPIES):
                query_copy(copy).wait_recv()

        unit = jnp.minimum(done, UNITS - 1)
        item, half = unit // HALVES, lax.rem(unit, HALVES)
        word = jnp.where(item >= 7, jnp.int32(item_words[1]), jnp.int32(item_words[0]))
        code = lax.shift_right_logical(word, lax.rem(item, 7) * 4) & 15
        head, group = code // 8, lax.rem(code, 8)
        now = ready_table.at(at)
        past = jnp.where(step == 0, 0, ready_table.at(jnp.maximum(at - 1, 0)))
        arrived = jnp.where(
            step >= ROUNDS, groups, jnp.where(stream >= jnp.where(head == 0, 1, 3), now, past)
        )
        empty = (group != DIAGONAL) & (group >= groups)
        open_now = (group == DIAGONAL) | (group < arrived) | empty
        open_now = open_now & (index >= jnp.where(head == 0, FIRST_STEP, SECOND_STEP))
        open_now = open_now & (done < UNITS)

        @pl.when(open_now & (group == DIAGONAL))
        def _():
            attend_own(head, half)

        @pl.when(open_now & (group != DIAGONAL) & (group < groups))
        def _():
            attend_group(head, group, half)

        return done + open_now.astype(jnp.int32)

    lax.fori_loop(0, STEPS, step_body, jnp.int32(0))

    for head in range(HEADS):
        o_ref[0, :, pl.ds(head * HEAD, HEAD)] = (summed[head] / total[head]).astype(jnp.bfloat16)

    def drain(step, carry):
        for direction in range(4):
            code = send_tables[direction].at(step)

            @pl.when(code != 1023)
            def _():
                for stream in range(4):
                    link_copy(direction, step, stream, code // 32, lax.rem(code, 32)).wait_send()
        return carry

    lax.fori_loop(0, ROUNDS, drain, 0)
    for stream in range(4):
        hop(stream).wait_send()
    for index in range(QUERY_COPIES):
        query_copy(index).wait_send()
    docs_copy.wait_send()


def body(queries, keys, values, modality, query_gain, tower_key_gain, doc_lengths):
    vmem = pl.BlockSpec(memory_space=pltpu.VMEM)
    dma = pltpu.SemaphoreType.DMA
    return pl.pallas_call(
        kernel,
        out_shape=jax.ShapeDtypeStruct(queries.shape, jnp.bfloat16),
        in_specs=[vmem] * 7,
        out_specs=vmem,
        scratch_shapes=[
            pltpu.VMEM((KV_HEADS, SLOTS, 2, ROWS, HEAD), jnp.bfloat16),
            pltpu.VMEM((KV_HEADS, ROWS, HEAD), jnp.bfloat16),
            pltpu.VMEM((HEADS, ROWS, HEAD), jnp.bfloat16),
            pltpu.VMEM((HEADS, ROWS, HEAD), jnp.bfloat16),
            pltpu.VMEM((8, HEAD), jnp.int32),
            pltpu.VMEM((8, HEAD), jnp.int32),
            pltpu.VMEM((WINDOW + 1, ROWS, HEAD), jnp.bfloat16),
            pltpu.VMEM((ROWS, HEAD), jnp.bfloat16),
            pltpu.VMEM((HEADS, ROWS, HEAD), jnp.float32),
            pltpu.VMEM((HEADS, ROWS, HEAD), jnp.float32),
            pltpu.VMEM((HEADS, ROWS, HEAD), jnp.float32),
            dma((4, ROUNDS, 4)),
            dma((4, ROUNDS, 4)),
            dma((4,)),
            dma((4,)),
            dma((QUERY_COPIES,)),
            dma((QUERY_COPIES,)),
            dma((2,)),
        ],
        compiler_params=pltpu.CompilerParams(
            collective_id=3, has_side_effects=True, vmem_limit_bytes=48 * 2**20
        ),
        name="relayed_attention",
    )(queries, keys, values, modality, query_gain, tower_key_gain, doc_lengths)


def solution(mesh):
    placed = (
        P("section", "ctx", "tp"),
        P("section", "ctx", "tp"),
        P("section", "ctx", "tp"),
        P("section", "ctx"),
        P(None, "tp"),
        P(None, "tp"),
        P("section", None),
    )
    return jax.shard_map(
        body, mesh=mesh, in_specs=placed, out_specs=P("section", "ctx", "tp"), check_vma=False
    )
```

time: 612 us -> 95.8 us (0.16)
  the two profiles are of different devices: /device:TPU:174 before, /device:TPU:6 now
where the time goes in v1:
time: 95.8 us; the launch traced here: 94.9 us
  Pallas kernels  88.3 us (92%)
  local copies, waits for them, and re-layouts  6.53 us (7%)
    pallas_call x1, Pallas kernels, body(): pl.pallas_call(kernel, out_shape=jax.ShapeDtypeStruct(queries.shape, jnp....  88.3 us
    unnamed x15, local copies, waits for them, and re-layouts  6.53 us

profile of v1, /device:TPU:6, one launch (start us, length us, event | category | flops | bytes accessed | tf_op | source)
XLA Modules:
  0.0 94.9 jit_solution(2573828486877812305)
XLA Ops:
  0.0 0.0 copy-start
  0.0 1.1 %copy-done = bf16[1,192,2048]{2,1,0:T(8,128)(2,1)S(1)} copy-done((bf16[1,192,2048]{2,1,0:T(8,128)(2,1)S(1)}, bf16[1,192,2048]{2,1,0:T(8,128)(2,1)}, u32[]{:S(2)}) %copy-start) | copy-done | bytes 786456
  1.1 0.0 copy-start.1
  1.1 0.9 copy-done.1
  2.0 0.0 copy-start.2
  2.0 0.9 copy-done.2
  2.9 0.0 copy-start.3
  2.9 0.7 copy-done.3
  3.6 0.0 copy-start.4
  3.6 0.7 copy-done.4
  4.3 0.0 copy-start.5
  4.3 0.7 copy-done.5
  5.0 0.0 copy-start.6
  5.0 0.7 copy-done.6
  5.7 88.3 %relayed_attention.1 = bf16[1,192,2048]{2,1,0:T(8,128)(2,1)S(1)} custom-call(bf16[1,192,2048]{2,1,0:T(8,128)(2,1)S(1)} %copy-done, bf16[1,192,256]{2,1,0:T(8,128)(2,1)S(1)} %copy-done.1, bf16[1,192,256]{2,1,0:T(8,128)(2,1)S(1)} %copy-done.2, s32[1,192]{1,0:T(1,128)S(1)} %copy-done.5, f32[2,2048]{1,0:T(2,128)S(1)} %copy-done.3, f32[2,256]{1,0:T(2,128)S(1)} %copy-done.4, ...), custom_call_target="tpu_custom_call" | custom-call | tf_op jit(solution)/shard_map/relayed_attention/pallas_call | solution.py:449
  94.0 0.9 copy.9
Async XLA Ops:
  0.0 1.1 %copy-start = (bf16[1,192,2048]{2,1,0:T(8,128)(2,1)S(1)}, bf16[1,192,2048]{2,1,0:T(8,128)(2,1)}, u32[]{:S(2)}) copy-start(bf16[1,192,2048]{2,1,0:T(8,128)(2,1)} %q_ref.1) | copy-start | bytes 2359300
  1.1 0.9 copy-start.1
  2.0 0.9 copy-start.2
  2.9 0.7 copy-start.3
  3.6 0.7 copy-start.4
  4.3 0.7 copy-start.5
  5.0 0.7 copy-start.6

commit v2 on v1

v2 whole, which is shorter than its diff:
```python
import functools

import jax
import jax.numpy as jnp
from jax import lax
from jax.experimental import pallas as pl
from jax.experimental.pallas import tpu as pltpu
from jax.sharding import PartitionSpec as P

MESH = pl.DeviceIdType.MESH
NT = (((1,), (1,)), ((), ()))
HEAD = 128
ROWS = 192
KV_HEADS = 2
GROUP = 8
HEADS = KV_HEADS * GROUP
BLOCKS = 32
WINDOW = 20
SLOTS = 32
OWN = 31
PER_GROUP = 4
GROUP_KEYS = PER_GROUP * ROWS
KEY_GROUPS = WINDOW // PER_GROUP
BIG = float(1 << 20)
LOG2E = 1.4426950408889634
EXP_SCALE = HEAD ** -0.5 * LOG2E
DIAGONAL = 7

SCHEDULE = (
    (
        0, 64, 129, 193, 258, 290, 322, 387, 419, 451, 516, 548, 580, 612, 645, 677, 709, 741, 774, 806,
        838, 870, 903, 935, 999, 1032, 1096, 1161, 1225, 1290, 1322, 1354, 1419, 1451, 1483, 1548, 1580,
        1612, 1677, 1709, 1741, 1806, 1870, 1935, 1967, 2064, 2128, 2193, 2257, 2322, 2386, 2451, 2515,
        2580, 2644, 2709, 2773, 2838, 2902, 2967, 3160, 3289, 3418, 3547, 3676, 3805, 3934,
    ),
    (
        192, 289, 321, 386, 427, 450, 484, 515, 549, 579, 613, 644, 685, 708, 742, 773, 805, 837, 871, 902,
        943, 1024, 1153, 1224, 1249, 1289, 1321, 1353, 1378, 1418, 1450, 1482, 1507, 1547, 1579, 1611,
        1636, 1676, 1708, 1740, 1765, 1805, 1869, 1894, 1934, 1966, 2023, 2056, 2120, 2185, 2256, 2281,
        2321, 2385, 2410, 2450, 2514, 2539, 2579, 2643, 2668, 2708, 2772, 2797, 2830, 2901, 2926, 2966,
        3055, 3152, 3288, 3313, 3362, 3417, 3442, 3546, 3571, 3620, 3675, 3700, 3749, 3804, 3829, 3878,
        3933, 3958, 4007, 4087,
    ),
    (
        128, 256, 297, 320, 356, 385, 426, 449, 485, 514, 555, 578, 614, 643, 684, 707, 743, 772, 804, 836,
        901, 942, 1025, 1154, 1217, 1250, 1283, 1352, 1379, 1410, 1449, 1481, 1508, 1539, 1578, 1610, 1637,
        1668, 1707, 1739, 1766, 1804, 1868, 1895, 1926, 1965, 2057, 2112, 2186, 2248, 2282, 2315, 2384,
        2411, 2444, 2513, 2540, 2578, 2642, 2669, 2707, 2771, 2798, 2829, 2900, 2927, 2965, 3047, 3144,
        3280, 3314, 3361, 3416, 3443, 3491, 3545, 3572, 3621, 3674, 3701, 3803, 3830, 3877, 3932, 3959,
        4079,
    ),
    (
        132, 228, 298, 357, 390, 425, 448, 486, 513, 554, 577, 615, 642, 683, 706, 771, 803, 835, 900, 941,
        1026, 1155, 1251, 1284, 1344, 1413, 1480, 1509, 1545, 1609, 1667, 1706, 1738, 1767, 1803, 1835,
        1867, 1925, 1964, 2058, 2187, 2240, 2283, 2316, 2376, 2412, 2449, 2512, 2541, 2574, 2641, 2670,
        2706, 2770, 2799, 2828, 2899, 2918, 2964, 3272, 3315, 3408, 3444, 3544, 3573, 3673, 3702, 3802,
        3831, 3876, 3931, 3951, 4085,
    ),
    (
        36, 165, 229, 294, 358, 391, 423, 487, 556, 576, 641, 674, 705, 770, 811, 834, 899, 940, 1027,
        1156, 1252, 1285, 1381, 1408, 1472, 1510, 1537, 1608, 1673, 1737, 1802, 1834, 1866, 1924, 1963,
        2059, 2188, 2284, 2317, 2369, 2413, 2446, 2504, 2542, 2569, 2640, 2671, 2705, 2769, 2790, 2834,
        2898, 2919, 2963, 3316, 3400, 3445, 3497, 3536, 3574, 3626, 3672, 3703, 3755, 3801, 3823, 3875,
        3930, 3950, 4013, 4084,
    ),
    (
        37, 166, 230, 295, 359, 640, 682, 704, 769, 810, 833, 898, 939, 1253, 1286, 1382, 1414, 1511, 1538,
        1665, 1736, 1794, 1865, 1930, 2060, 2189, 2285, 2318, 2372, 2414, 2445, 2496, 2543, 2573, 2632,
        2697, 2768, 2791, 2833, 2897, 2922, 2962, 3108, 3237, 3317, 3446, 3495, 3528, 3575, 3664, 3695,
        3746, 3800, 3825, 3929, 4012, 4083,
    ),
    (
        38, 167, 231, 832, 897, 1158, 1254, 1287, 1383, 1728, 1801, 1864, 1929, 2061, 2190, 2286, 2415,
        2760, 2896, 2961, 3109, 3318, 3447, 3567, 3792, 3928, 4011,
    ),
    (
        39, 1030, 1255, 1856, 1923, 2062, 2191, 2287, 2888, 3239, 3319, 3920,
    ),
    (
        2063, 3111,
    ),
)
ROUNDS = len(SCHEDULE)


def neighbour(chip, direction):
    x, z = divmod(chip, 8)
    return (
        ((x + 1) % 4) * 8 + z,
        ((x + 3) % 4) * 8 + z,
        chip + 1,
        chip - 1,
    )[direction]


def relay_tables():
    slot = [{chip: OWN} for chip in range(BLOCKS)]
    count = [0] * BLOCKS
    spare = [WINDOW] * BLOCKS
    sends = [[[1023] * ROUNDS for _ in range(4)] for _ in range(BLOCKS)]
    takes = [[[31] * ROUNDS for _ in range(4)] for _ in range(BLOCKS)]
    ready = [[0] * ROUNDS for _ in range(BLOCKS)]
    for step, entries in enumerate(SCHEDULE):
        known = [dict(held) for held in slot]
        for entry in entries:
            link, block = divmod(entry, 32)
            sender, direction = divmod(link, 4)
            target = neighbour(sender, direction)
            if max(0, target - WINDOW) <= block < target:
                place = count[target]
                count[target] += 1
            else:
                place = spare[target]
                spare[target] += 1
            assert place < OWN and block not in slot[target]
            slot[target][block] = place
            sends[sender][direction][step] = known[sender][block] * 32 + place
            takes[target][direction][step] = place
        for chip in range(BLOCKS):
            ready[chip][step] = count[chip] // PER_GROUP
    for chip in range(BLOCKS):
        assert count[chip] == min(chip, WINDOW)
        ready[chip][ROUNDS - 1] = -(-count[chip] // PER_GROUP)
    owners = [[31] * WINDOW for _ in range(BLOCKS)]
    for chip in range(BLOCKS):
        for block, place in slot[chip].items():
            if place < WINDOW:
                owners[chip][place] = block
    return sends, takes, ready, owners, count


def packed(values, bits):
    per = 30 // bits
    return [
        sum(value << (bits * i) for i, value in enumerate(values[at : at + per]))
        for at in range(0, len(values), per)
    ]


def chosen(chip, per_chip):
    result = jnp.int32(per_chip[0])
    for index in range(1, len(per_chip)):
        if per_chip[index] != per_chip[0]:
            result = jnp.where(chip == index, jnp.int32(per_chip[index]), result)
    return result


class Table:
    def __init__(self, chip, per_chip, bits):
        self.bits = bits
        self.per = 30 // bits
        rows = [packed(values, bits) for values in per_chip]
        self.words = [chosen(chip, column) for column in zip(*rows)]

    def at(self, index):
        word = self.words[0]
        for place in range(1, len(self.words)):
            word = jnp.where(index >= place * self.per, self.words[place], word)
        shift = lax.rem(index, self.per) * self.bits
        return lax.shift_right_logical(word, shift) & ((1 << self.bits) - 1)


TILE_HEADS = 4
TILE_ROWS = TILE_HEADS * ROWS
TILES = GROUP // TILE_HEADS
STREAMS = 2 * KV_HEADS
FIRST_STEP = 5
SECOND_STEP = 9
CHUNKS = ROUNDS * KV_HEADS + KV_HEADS * (KEY_GROUPS + 1)
QUERY_COPIES = 8


def kernel(
    q_hbm, k_hbm, v_hbm, modality_hbm, q_gain_hbm, k_gain_hbm, docs_hbm, o_ref,
    q_in, k_in, modality, q_gain, k_gain, docs_own,
    kv, key_stage, query_stage, queries, docs_stage, docs_in, key_docs, query_docs,
    peak, total, summed,
    load_sems, link_send, link_recv, hop_send, hop_recv, query_send, query_recv, docs_sems,
):
    loads = [
        pltpu.make_async_copy(source, target, load_sems.at[index])
        for index, (source, target) in enumerate(
            (
                (k_hbm, k_in), (modality_hbm, modality), (k_gain_hbm, k_gain), (docs_hbm, docs_own),
                (q_gain_hbm, q_gain), (q_hbm, q_in),
            )
        )
    ]
    for load in loads:
        load.start()

    section = lax.axis_index("section")
    chip = lax.axis_index("ctx")
    part = lax.axis_index("tp")
    x, z = chip // 8, lax.rem(chip, 8)
    after = (lax.rem(section + 1, 4), chip, part)
    before = (lax.rem(section + 3, 4), chip, part)
    around = (
        (section, lax.rem(x + 1, 4) * 8 + z, part),
        (section, lax.rem(x + 3, 4) * 8 + z, part),
        (section, x * 8 + jnp.minimum(z + 1, 7), part),
        (section, x * 8 + jnp.maximum(z - 1, 0), part),
    )
    exists = (None, None, z < 7, z > 0)

    barrier = pltpu.get_barrier_semaphore()
    for device in (after, before, around[0], around[1]):
        pl.semaphore_signal(barrier, inc=1, device_id=device, device_id_type=MESH)
    for direction in (2, 3):
        @pl.when(exists[direction])
        def _():
            pl.semaphore_signal(barrier, inc=1, device_id=around[direction], device_id_type=MESH)

    for load in loads[:3]:
        load.wait()
    diagonal = lax.broadcasted_iota(jnp.int32, (ROWS, ROWS), 0) == lax.broadcasted_iota(
        jnp.int32, (ROWS, ROWS), 1
    )
    towers = jnp.sum(
        jnp.where(diagonal, modality[0:1, :].astype(jnp.float32), 0.0), axis=1, keepdims=True
    )
    image = jnp.broadcast_to(towers, (ROWS, HEAD)) > 0.5

    def scaled(values, gain_ref, channels):
        gains = jnp.where(image, gain_ref[1:2, channels], gain_ref[0:1, channels])
        return (values.astype(jnp.float32) * gains).astype(jnp.bfloat16)

    for head in range(KV_HEADS):
        channels = pl.ds(head * HEAD, HEAD)
        key_stage[head] = scaled(k_in[0, :, channels], k_gain, channels)

    pl.semaphore_wait(barrier, 4 + (z < 7).astype(jnp.int32) + (z > 0).astype(jnp.int32))

    def hop(head, kind):
        if kind == 0:
            source = key_stage.at[head]
        else:
            source = v_hbm.at[0, :, pl.ds(head * HEAD, HEAD)]
        return pltpu.make_async_remote_copy(
            src_ref=source, dst_ref=kv.at[head, OWN, kind],
            send_sem=hop_send.at[head, kind], recv_sem=hop_recv.at[head, kind],
            device_id=after, device_id_type=MESH,
        )

    for head in range(KV_HEADS):
        for kind in range(2):
            hop(head, kind).start()

    loads[3].wait()
    docs_stage[...] = jnp.zeros_like(docs_stage)
    docs_stage[0:1, 0:16] = docs_own[...]
    docs_copy = pltpu.make_async_remote_copy(
        src_ref=docs_stage, dst_ref=docs_in, send_sem=docs_sems.at[0], recv_sem=docs_sems.at[1],
        device_id=after, device_id_type=MESH,
    )
    docs_copy.start()

    sends, takes, ready, owners, count = relay_tables()
    send_tables = [Table(chip, [sends[c][d] for c in range(BLOCKS)], 10) for d in range(4)]
    take_tables = [Table(chip, [takes[c][d] for c in range(BLOCKS)], 5) for d in range(4)]
    ready_table = Table(chip, ready, 3)
    owner_table = Table(chip, owners, 5)
    arrivals = jnp.minimum(chip, WINDOW)
    groups = (arrivals + PER_GROUP - 1) // PER_GROUP

    def link_copy(direction, step, head, kind, source, target):
        return pltpu.make_async_remote_copy(
            src_ref=kv.at[head, source, kind], dst_ref=kv.at[head, target, kind],
            send_sem=link_send.at[direction, step, 2 * head + kind],
            recv_sem=link_recv.at[direction, step, 2 * head + kind],
            device_id=around[direction], device_id_type=MESH,
        )

    def start_round(codes, step, head, kind):
        for direction in range(4):
            code = codes[direction]

            @pl.when(code != 1023)
            def _():
                link_copy(direction, step, head, kind, code // 32, lax.rem(code, 32)).start()

    def take_round(places, step, head, kind):
        for direction in range(4):
            place = places[direction]

            @pl.when(place != 31)
            def _():
                link_copy(direction, step, head, kind, place, place).wait_recv()

    def query_copy(index):
        heads = pl.ds(index * (HEADS // QUERY_COPIES), HEADS // QUERY_COPIES)
        return pltpu.make_async_remote_copy(
            src_ref=query_stage.at[heads], dst_ref=queries.at[heads],
            send_sem=query_send.at[index], recv_sem=query_recv.at[index],
            device_id=after, device_id_type=MESH,
        )

    loads[4].wait()
    loads[5].wait()

    def scale_queries(kv_head):
        for head in range(kv_head * GROUP, (kv_head + 1) * GROUP):
            channels = pl.ds(head * HEAD, HEAD)
            query_stage[head] = scaled(q_in[0, :, channels], q_gain, channels)

    scale_queries(0)
    for index in range(QUERY_COPIES // 2):
        query_copy(index).start()
    first_codes = [table.at(0) for table in send_tables]
    for head in range(KV_HEADS):
        for kind in range(2):
            hop(head, kind).wait_recv()
            start_round(first_codes, 0, head, kind)
    scale_queries(1)
    for index in range(QUERY_COPIES // 2, QUERY_COPIES):
        query_copy(index).start()

    def clear(place, carry):
        for head in range(KV_HEADS):
            kv[head, place] = jnp.zeros((2, ROWS, HEAD), jnp.bfloat16)
        return carry

    lax.fori_loop(arrivals, groups * PER_GROUP, clear, 0)

    docs_copy.wait_recv()
    lengths = docs_in[0:1, :].astype(jnp.float32)
    square = (HEAD, HEAD)
    down = lax.broadcasted_iota(jnp.int32, square, 0)
    across = lax.broadcasted_iota(jnp.int32, square, 1)
    column = jnp.sum(jnp.where(down == across, lengths, 0.0), axis=1, keepdims=True)
    first = jnp.sum(jnp.where(down < across, column, 0.0), axis=0, keepdims=True)
    lane = lax.broadcasted_iota(jnp.int32, (1, HEAD), 1)
    last = jnp.where(lane == 15, 1e9, first + lengths)
    first = jnp.where(lane < 16, first, jnp.where(lane == 16, -1e9, 1e9))
    last = jnp.where(lane < 16, last, jnp.where(lane == 16, 0.0, 1e9))
    inner = lax.broadcasted_iota(jnp.int32, (ROWS, HEAD), 0)

    def members(block):
        places = (inner + block * ROWS).astype(jnp.float32)
        return (places >= first) & (places < last)

    def mark(place, carry):
        block = jnp.where(place < arrivals, owner_table.at(place), -1)
        key_docs[place] = jnp.where(members(block), 1.0, 0.0).astype(jnp.bfloat16)
        return carry

    lax.fori_loop(0, groups * PER_GROUP, mark, 0)
    own_members = members(chip)
    key_docs[WINDOW] = jnp.where(own_members, 1.0, 0.0).astype(jnp.bfloat16)
    query_docs[...] = jnp.where(own_members, 0.0, -BIG).astype(jnp.bfloat16)

    def tiles_of(head, keys, values, size, fresh):
        keys, marked = keys
        keys = jnp.concatenate([keys.reshape(size, HEAD), marked.reshape(size, HEAD)], axis=1)
        values = jnp.concatenate(
            [values.reshape(size, HEAD), jnp.ones((size, HEAD), jnp.bfloat16)], axis=1
        )
        marks = jnp.concatenate([query_docs[...]] * TILE_HEADS, axis=0)
        shape = (TILE_HEADS, ROWS, HEAD)

        def rows_of(tile):
            return pl.ds(head * GROUP + tile * TILE_HEADS, TILE_HEADS)

        def score(tile):
            rows = queries[rows_of(tile)].reshape(TILE_ROWS, HEAD)
            rows = jnp.concatenate([rows, marks], axis=1)
            return lax.dot_general(rows, keys, NT, preferred_element_type=jnp.float32)

        scores = {0: score(0)}
        held = {}
        for tile in range(TILES + 1):
            if tile + 1 < TILES:
                scores[tile + 1] = score(tile + 1)
            if tile >= 1:
                weights, shrink = held.pop(tile - 1)
                rows = rows_of(tile - 1)
                mixed = jnp.dot(weights, values, preferred_element_type=jnp.float32)
                if fresh:
                    summed[rows] = mixed[:, :HEAD].reshape(shape)
                    total[rows] = mixed[:, HEAD:].reshape(shape)
                else:
                    summed[rows] = summed[rows] * shrink + mixed[:, :HEAD].reshape(shape)
                    total[rows] = total[rows] * shrink + mixed[:, HEAD:].reshape(shape)
            if tile < TILES:
                rows = rows_of(tile)
                now = scores.pop(tile)
                if fresh:
                    below = lax.broadcasted_iota(jnp.int32, shape[:1] + (ROWS, ROWS), 1)
                    below = below >= lax.broadcasted_iota(jnp.int32, shape[:1] + (ROWS, ROWS), 2)
                    now = jnp.where(below, now.reshape(shape[:1] + (ROWS, ROWS)), -1e30)
                    now = now.reshape(TILE_ROWS, ROWS)
                    new = jnp.broadcast_to(
                        jnp.max(now, axis=1, keepdims=True), (TILE_ROWS, HEAD)
                    )
                    shrink = None
                else:
                    old = peak[rows].reshape(TILE_ROWS, HEAD)
                    new = jnp.maximum(old, jnp.max(now, axis=1, keepdims=True))
                    shrink = jnp.exp2((old - new) * EXP_SCALE).reshape(shape)
                weights = jnp.exp2((now - new[:, 0:1]) * EXP_SCALE).astype(jnp.bfloat16)
                peak[rows] = new.reshape(shape)
                held[tile] = (weights, shrink)

    def step_body(index, done):
        step, stream = index // KV_HEADS, lax.rem(index, KV_HEADS)
        at = jnp.minimum(step, ROUNDS - 1)
        later = jnp.minimum(step + 1, ROUNDS - 1)

        @pl.when(step < ROUNDS)
        def _():
            places = [table.at(at) for table in take_tables]
            codes = [
                jnp.where(step + 1 < ROUNDS, table.at(later), 1023) for table in send_tables
            ]
            for kind in range(2):
                take_round(places, at, stream, kind)
                start_round(codes, later, stream, kind)

        @pl.when(index == FIRST_STEP)
        def _():
            for copy in range(QUERY_COPIES // 2):
                query_copy(copy).wait_recv()

        @pl.when(index == SECOND_STEP)
        def _():
            for copy in range(QUERY_COPIES // 2, QUERY_COPIES):
                query_copy(copy).wait_recv()

        now = jnp.where(step >= ROUNDS, groups, ready_table.at(at))
        past = jnp.where(step == 0, 0, ready_table.at(jnp.maximum(at - 1, 0)))
        past = jnp.where(step >= ROUNDS, groups, past)
        open_first = jnp.where(index >= FIRST_STEP, 1 + now, 0) - done[0]
        open_second = jnp.where(
            index >= SECOND_STEP, 1 + jnp.where(stream == 1, now, past), 0
        ) - done[1]
        pick_first = (open_first > 0) & ((done[0] <= done[1]) | (open_second <= 0))
        pick_second = (open_second > 0) & jnp.logical_not(pick_first)
        head = pick_second.astype(jnp.int32)
        place = jnp.where(pick_second, done[1], done[0])
        some = pick_first | pick_second

        @pl.when(some & (place == 0))
        def _():
            tiles_of(head, (kv[head, OWN, 0], key_docs[WINDOW]), kv[head, OWN, 1], ROWS, True)

        @pl.when(some & (place > 0))
        def _():
            slots = pl.ds((place - 1) * PER_GROUP, PER_GROUP)
            tiles_of(
                head, (kv[head, slots, 0], key_docs[slots]), kv[head, slots, 1], GROUP_KEYS, False
            )

        return (done[0] + pick_first.astype(jnp.int32), done[1] + pick_second.astype(jnp.int32))

    lax.fori_loop(0, CHUNKS, step_body, (jnp.int32(0), jnp.int32(0)))

    for head in range(HEADS):
        o_ref[0, :, pl.ds(head * HEAD, HEAD)] = (summed[head] / total[head]).astype(jnp.bfloat16)

    def drain(step, carry):
        for direction in range(4):
            code = send_tables[direction].at(step)

            @pl.when(code != 1023)
            def _():
                for head in range(KV_HEADS):
                    for kind in range(2):
                        link_copy(
                            direction, step, head, kind, code // 32, lax.rem(code, 32)
                        ).wait_send()
        return carry

    lax.fori_loop(0, ROUNDS, drain, 0)
    for head in range(KV_HEADS):
        hop(head, 0).wait_send()
        hop(head, 1).wait_send()
    for index in range(QUERY_COPIES):
        query_copy(index).wait_send()
    docs_copy.wait_send()


def body(queries, keys, values, modality, query_gain, tower_key_gain, doc_lengths):
    vmem = pl.BlockSpec(memory_space=pltpu.VMEM)
    dma = pltpu.SemaphoreType.DMA
    return pl.pallas_call(
        kernel,
        out_shape=jax.ShapeDtypeStruct(queries.shape, jnp.bfloat16),
        in_specs=[pl.BlockSpec(memory_space=pltpu.HBM)] * 7,
        out_specs=vmem,
        scratch_shapes=[
            pltpu.VMEM(queries.shape, jnp.bfloat16),
            pltpu.VMEM(keys.shape, jnp.bfloat16),
            pltpu.VMEM(modality.shape, jnp.int32),
            pltpu.VMEM(query_gain.shape, jnp.float32),
            pltpu.VMEM(tower_key_gain.shape, jnp.float32),
            pltpu.VMEM(doc_lengths.shape, jnp.int32),
            pltpu.VMEM((KV_HEADS, SLOTS, 2, ROWS, HEAD), jnp.bfloat16),
            pltpu.VMEM((KV_HEADS, ROWS, HEAD), jnp.bfloat16),
            pltpu.VMEM((HEADS, ROWS, HEAD), jnp.bfloat16),
            pltpu.VMEM((HEADS, ROWS, HEAD), jnp.bfloat16),
            pltpu.VMEM((8, HEAD), jnp.int32),
            pltpu.VMEM((8, HEAD), jnp.int32),
            pltpu.VMEM((WINDOW + 1, ROWS, HEAD), jnp.bfloat16),
            pltpu.VMEM((ROWS, HEAD), jnp.bfloat16),
            pltpu.VMEM((HEADS, ROWS, HEAD), jnp.float32),
            pltpu.VMEM((HEADS, ROWS, HEAD), jnp.float32),
            pltpu.VMEM((HEADS, ROWS, HEAD), jnp.float32),
            dma((6,)),
            dma((4, ROUNDS, STREAMS)),
            dma((4, ROUNDS, STREAMS)),
            dma((KV_HEADS, 2)),
            dma((KV_HEADS, 2)),
            dma((QUERY_COPIES,)),
            dma((QUERY_COPIES,)),
            dma((2,)),
        ],
        compiler_params=pltpu.CompilerParams(
            collective_id=3, has_side_effects=True, vmem_limit_bytes=63 * 2**20
        ),
        name="relayed_attention",
    )(queries, keys, values, modality, query_gain, tower_key_gain, doc_lengths)


def solution(mesh):
    placed = (
        P("section", "ctx", "tp"),
        P("section", "ctx", "tp"),
        P("section", "ctx", "tp"),
        P("section", "ctx"),
        P(None, "tp"),
        P(None, "tp"),
        P("section", None),
    )
    return jax.shard_map(
        body, mesh=mesh, in_specs=placed, out_specs=P("section", "ctx", "tp"), check_vma=False
    )
```

time: 95.8 us -> 62.4 us (0.65)
  Pallas kernels: 88.3 us -> 60.2 us
  local copies, waits for them, and re-layouts: 6.53 us -> 2.09 us
    pallas_call x1, Pallas kernels: 88.3 us -> 60.2 us  [body(): pl.pallas_call(kernel, out_shape=jax.ShapeDtypeStruct(queries.shape, jnp....]
    unnamed x15 -> x1, local copies, waits for them, and re-layouts: 6.53 us -> 2.09 us
where the time goes in v2:
time: 62.4 us; the launch traced here: 62.3 us
  Pallas kernels  60.2 us (96%)
  local copies, waits for them, and re-layouts  2.09 us (3%)
    pallas_call x1, Pallas kernels, body(): pl.pallas_call(kernel, out_shape=jax.ShapeDtypeStruct(queries.shape, jnp....  60.2 us
    unnamed x1, local copies, waits for them, and re-layouts  2.09 us

profile of v2, /device:TPU:6, one launch (start us, length us, event | category | flops | bytes accessed | tf_op | source)
XLA Modules:
  0.0 62.3 jit_solution(12486226070987866581)
XLA Ops:
  0.0 60.2 %relayed_attention.1 = bf16[1,192,2048]{2,1,0:T(8,128)(2,1)} custom-call(bf16[1,192,2048]{2,1,0:T(8,128)(2,1)} %q_hbm.1, bf16[1,192,256]{2,1,0:T(8,128)(2,1)} %k_hbm.1, bf16[1,192,256]{2,1,0:T(8,128)(2,1)} %v_hbm.1, s32[1,192]{1,0:T(1,128)} %modality_hbm.1, f32[2,2048]{1,0:T(2,128)} %q_gain_hbm.1, f32[2,256]{1,0:T(2,128)} %k_gain_hbm.1, s32[1,16]{1,0:T(1,128)} %docs_hbm.1), custom_call_target="tpu_custom_call" | custom-call | tf_op jit(solution)/shard_map/relayed_attention/pallas_call | solution.py:485
  60.2 2.1 %copy.9 = bf16[1,192,2048]{2,1,0:T(8,128)(2,1)} copy(bf16[1,192,2048]{2,1,0:T(8,128)(2,1)} %relayed_attention.1) | data formatting | bytes 1572864

commit v3 on v2

--- a/solution.py
+++ b/solution.py
@@ -28,56 +28,54 @@
 
 SCHEDULE = (
     (
-        0, 64, 129, 193, 258, 290, 322, 387, 419, 451, 516, 548, 580, 612, 645, 677, 709, 741, 774, 806,
-        838, 870, 903, 935, 999, 1032, 1096, 1161, 1225, 1290, 1322, 1354, 1419, 1451, 1483, 1548, 1580,
-        1612, 1677, 1709, 1741, 1806, 1870, 1935, 1967, 2064, 2128, 2193, 2257, 2322, 2386, 2451, 2515,
-        2580, 2644, 2709, 2773, 2838, 2902, 2967, 3160, 3289, 3418, 3547, 3676, 3805, 3934,
-    ),
-    (
-        192, 289, 321, 386, 427, 450, 484, 515, 549, 579, 613, 644, 685, 708, 742, 773, 805, 837, 871, 902,
-        943, 1024, 1153, 1224, 1249, 1289, 1321, 1353, 1378, 1418, 1450, 1482, 1507, 1547, 1579, 1611,
-        1636, 1676, 1708, 1740, 1765, 1805, 1869, 1894, 1934, 1966, 2023, 2056, 2120, 2185, 2256, 2281,
-        2321, 2385, 2410, 2450, 2514, 2539, 2579, 2643, 2668, 2708, 2772, 2797, 2830, 2901, 2926, 2966,
-        3055, 3152, 3288, 3313, 3362, 3417, 3442, 3546, 3571, 3620, 3675, 3700, 3749, 3804, 3829, 3878,
-        3933, 3958, 4007, 4087,
-    ),
-    (
-        128, 256, 297, 320, 356, 385, 426, 449, 485, 514, 555, 578, 614, 643, 684, 707, 743, 772, 804, 836,
-        901, 942, 1025, 1154, 1217, 1250, 1283, 1352, 1379, 1410, 1449, 1481, 1508, 1539, 1578, 1610, 1637,
-        1668, 1707, 1739, 1766, 1804, 1868, 1895, 1926, 1965, 2057, 2112, 2186, 2248, 2282, 2315, 2384,
-        2411, 2444, 2513, 2540, 2578, 2642, 2669, 2707, 2771, 2798, 2829, 2900, 2927, 2965, 3047, 3144,
-        3280, 3314, 3361, 3416, 3443, 3491, 3545, 3572, 3621, 3674, 3701, 3803, 3830, 3877, 3932, 3959,
-        4079,
-    ),
-    (
-        132, 228, 298, 357, 390, 425, 448, 486, 513, 554, 577, 615, 642, 683, 706, 771, 803, 835, 900, 941,
-        1026, 1155, 1251, 1284, 1344, 1413, 1480, 1509, 1545, 1609, 1667, 1706, 1738, 1767, 1803, 1835,
-        1867, 1925, 1964, 2058, 2187, 2240, 2283, 2316, 2376, 2412, 2449, 2512, 2541, 2574, 2641, 2670,
-        2706, 2770, 2799, 2828, 2899, 2918, 2964, 3272, 3315, 3408, 3444, 3544, 3573, 3673, 3702, 3802,
-        3831, 3876, 3931, 3951, 4085,
-    ),
-    (
-        36, 165, 229, 294, 358, 391, 423, 487, 556, 576, 641, 674, 705, 770, 811, 834, 899, 940, 1027,
-        1156, 1252, 1285, 1381, 1408, 1472, 1510, 1537, 1608, 1673, 1737, 1802, 1834, 1866, 1924, 1963,
-        2059, 2188, 2284, 2317, 2369, 2413, 2446, 2504, 2542, 2569, 2640, 2671, 2705, 2769, 2790, 2834,
-        2898, 2919, 2963, 3316, 3400, 3445, 3497, 3536, 3574, 3626, 3672, 3703, 3755, 3801, 3823, 3875,
-        3930, 3950, 4013, 4084,
-    ),
-    (
-        37, 166, 230, 295, 359, 640, 682, 704, 769, 810, 833, 898, 939, 1253, 1286, 1382, 1414, 1511, 1538,
-        1665, 1736, 1794, 1865, 1930, 2060, 2189, 2285, 2318, 2372, 2414, 2445, 2496, 2543, 2573, 2632,
-        2697, 2768, 2791, 2833, 2897, 2922, 2962, 3108, 3237, 3317, 3446, 3495, 3528, 3575, 3664, 3695,
-        3746, 3800, 3825, 3929, 4012, 4083,
-    ),
-    (
-        38, 167, 231, 832, 897, 1158, 1254, 1287, 1383, 1728, 1801, 1864, 1929, 2061, 2190, 2286, 2415,
-        2760, 2896, 2961, 3109, 3318, 3447, 3567, 3792, 3928, 4011,
-    ),
-    (
-        39, 1030, 1255, 1856, 1923, 2062, 2191, 2287, 2888, 3239, 3319, 3920,
-    ),
-    (
-        2063, 3111,
+        0, 32, 64, 161, 193, 225, 322, 354, 386, 483, 515, 547, 611, 644, 676, 708, 805, 837, 869, 933,
+        966, 998, 1030, 1127, 1159, 1255, 1288, 1320, 1352, 1449, 1481, 1513, 1545, 1610, 1642, 1674, 1771,
+        1803, 1835, 1899, 1932, 1964, 1996, 2028, 2093, 2125, 2157, 2254, 2318, 2382, 2415, 2447, 2576,
+        2640, 2737, 2801, 2833, 2898, 2962, 3059, 3123, 3187, 3220, 3284, 3381, 3445, 3509, 3542, 3606,
+        3703, 3831, 3928, 4089, 4250, 4411, 4572, 4733, 4894,
+    ),
+    (
+        40, 163, 201, 224, 259, 321, 362, 385, 485, 523, 546, 613, 643, 675, 707, 807, 845, 868, 935, 965,
+        997, 1029, 1126, 1167, 1289, 1321, 1344, 1451, 1512, 1537, 1609, 1641, 1673, 1698, 1772, 1802,
+        1834, 1934, 1963, 1995, 2062, 2092, 2124, 2156, 2253, 2317, 2374, 2414, 2446, 2577, 2632, 2739,
+        2800, 2897, 2961, 3018, 3058, 3122, 3157, 3219, 3283, 3383, 3444, 3501, 3534, 3605, 3702, 3823,
+        3872, 3920, 4033, 4088, 4194, 4249, 4306, 4355, 4410, 4516, 4571, 4612, 4677, 4732, 4838, 4893,
+        4950, 4999, 5079,
+    ),
+    (
+        3, 41, 165, 197, 261, 320, 361, 384, 487, 519, 545, 615, 642, 683, 706, 803, 844, 867, 909, 964,
+        996, 1028, 1125, 1166, 1281, 1442, 1507, 1538, 1614, 1646, 1672, 1710, 1765, 1801, 1833, 1930,
+        1994, 2054, 2091, 2123, 2155, 2183, 2252, 2316, 2342, 2406, 2445, 2503, 2570, 2624, 2731, 2785,
+        2827, 2901, 2946, 2997, 3052, 3121, 3149, 3214, 3282, 3375, 3443, 3503, 3540, 3604, 3622, 3701,
+        3783, 3922, 4080, 4196, 4248, 4292, 4409, 4515, 4570, 4630, 4731, 4759, 4837, 4892, 4910, 5071,
+    ),
+    (
+        5, 37, 167, 199, 263, 366, 430, 481, 521, 544, 641, 685, 705, 802, 843, 866, 963, 995, 1027, 1124,
+        1165, 1283, 1443, 1509, 1608, 1638, 1664, 1702, 1768, 1800, 1832, 1863, 1929, 1993, 2022, 2090,
+        2122, 2154, 2181, 2251, 2283, 2315, 2340, 2405, 2444, 2571, 2634, 2741, 2784, 2837, 2893, 2916,
+        2960, 2989, 3057, 3074, 3106, 3151, 3217, 3281, 3316, 3378, 3442, 3462, 3539, 3603, 3623, 3700,
+        3791, 3876, 3912, 4037, 4075, 4115, 4240, 4278, 4359, 4408, 4428, 4523, 4569, 4599, 4686, 4730,
+        4751, 4836, 4891, 4916, 5077,
+    ),
+    (
+        7, 39, 206, 270, 358, 422, 520, 684, 704, 801, 833, 865, 962, 1003, 1026, 1123, 1164, 1282, 1446,
+        1542, 1607, 1668, 1700, 1770, 1824, 1921, 1992, 2089, 2153, 2250, 2282, 2314, 2404, 2443, 2581,
+        2596, 2628, 2733, 2789, 2829, 2895, 2944, 2991, 3060, 3120, 3156, 3209, 3266, 3302, 3377, 3441,
+        3463, 3538, 3602, 3620, 3699, 3877, 3914, 4039, 4071, 4118, 4204, 4246, 4268, 4361, 4400, 4439,
+        4527, 4568, 4590, 4729, 4754, 4835, 4890, 4915, 5005, 5069,
+    ),
+    (
+        46, 198, 262, 522, 842, 864, 961, 1002, 1025, 1122, 1163, 1286, 1454, 1550, 1761, 1920, 1984, 2088,
+        2152, 2242, 2313, 2403, 2573, 2735, 2790, 2831, 2888, 2948, 2996, 3053, 3112, 3139, 3210, 3280,
+        3369, 3433, 3461, 3537, 3601, 3619, 3698, 3879, 4044, 4083, 4108, 4203, 4245, 4279, 4366, 4392,
+        4436, 4525, 4560, 4591, 4673, 4728, 4757, 4889, 4918, 5004, 5068,
+    ),
+    (
+        38, 960, 1024, 1121, 1294, 2248, 2312, 2410, 2575, 2740, 2836, 3440, 3593, 3697, 3884, 4119, 4720,
+        4888, 5003,
+    ),
+    (
+        1120, 2408, 2580, 3600, 4880,
     ),
 )
 ROUNDS = len(SCHEDULE)
@@ -90,6 +88,7 @@
         ((x + 3) % 4) * 8 + z,
         chip + 1,
         chip - 1,
+        chip - 2,
     )[direction]
 
 
@@ -97,14 +96,15 @@
     slot = [{chip: OWN} for chip in range(BLOCKS)]
     count = [0] * BLOCKS
     spare = [WINDOW] * BLOCKS
-    sends = [[[1023] * ROUNDS for _ in range(4)] for _ in range(BLOCKS)]
-    takes = [[[31] * ROUNDS for _ in range(4)] for _ in range(BLOCKS)]
+    sends = [[[1023] * ROUNDS for _ in range(DIRECTIONS)] for _ in range(BLOCKS)]
+    takes = [[[31] * ROUNDS for _ in range(DIRECTIONS)] for _ in range(BLOCKS)]
     ready = [[0] * ROUNDS for _ in range(BLOCKS)]
     for step, entries in enumerate(SCHEDULE):
         known = [dict(held) for held in slot]
         for entry in entries:
             link, block = divmod(entry, 32)
-            sender, direction = divmod(link, 4)
+            sender, direction = divmod(link, DIRECTIONS)
+            assert direction < 4 or step < FAR_ROUNDS
             target = neighbour(sender, direction)
             if max(0, target - WINDOW) <= block < target:
                 place = count[target]
@@ -164,18 +164,24 @@
 TILE_ROWS = TILE_HEADS * ROWS
 TILES = GROUP // TILE_HEADS
 STREAMS = 2 * KV_HEADS
-FIRST_STEP = 5
-SECOND_STEP = 9
+FORWARD_STEP = 0
+FORWARD_STEP_2 = 3
+FIRST_STEP = 2
+SECOND_STEP = 4
 CHUNKS = ROUNDS * KV_HEADS + KV_HEADS * (KEY_GROUPS + 1)
-QUERY_COPIES = 8
+QUERY_COPIES = 6
+ROUND_HEADS = 4
+SPLIT = 4
+DIRECTIONS = 5
+FAR_ROUNDS = 3
 
 
 def kernel(
     q_hbm, k_hbm, v_hbm, modality_hbm, q_gain_hbm, k_gain_hbm, docs_hbm, o_ref,
     q_in, k_in, modality, q_gain, k_gain, docs_own,
     kv, key_stage, query_stage, queries, docs_stage, docs_in, key_docs, query_docs,
-    peak, total, summed,
-    load_sems, link_send, link_recv, hop_send, hop_recv, query_send, query_recv, docs_sems,
+    peak, total, summed, detour,
+    load_sems, link_send, link_recv, whole_send, whole_recv, detour_send, detour_recv, hop_send, hop_recv, query_send, query_recv, docs_sems,
 ):
     loads = [
         pltpu.make_async_copy(source, target, load_sems.at[index])
@@ -200,16 +206,23 @@
         (section, lax.rem(x + 3, 4) * 8 + z, part),
         (section, x * 8 + jnp.minimum(z + 1, 7), part),
         (section, x * 8 + jnp.maximum(z - 1, 0), part),
+        (section, x * 8 + jnp.maximum(z - 2, 0), part),
     )
-    exists = (None, None, z < 7, z > 0)
+    further = (section, x * 8 + jnp.minimum(z + 2, 7), part)
 
     barrier = pltpu.get_barrier_semaphore()
     for device in (after, before, around[0], around[1]):
         pl.semaphore_signal(barrier, inc=1, device_id=device, device_id_type=MESH)
-    for direction in (2, 3):
-        @pl.when(exists[direction])
-        def _():
-            pl.semaphore_signal(barrier, inc=1, device_id=around[direction], device_id_type=MESH)
+    near = ((around[2], z < 7), (around[3], z > 0))
+    if FAR_ROUNDS:
+        near += ((around[4], z > 1), (further, z < 6))
+    expected = jnp.int32(4)
+    for device, exists in near:
+        expected += exists.astype(jnp.int32)
+
+        @pl.when(exists)
+        def _():
+            pl.semaphore_signal(barrier, inc=1, device_id=device, device_id_type=MESH)
 
     for load in loads[:3]:
         load.wait()
@@ -229,7 +242,7 @@
         channels = pl.ds(head * HEAD, HEAD)
         key_stage[head] = scaled(k_in[0, :, channels], k_gain, channels)
 
-    pl.semaphore_wait(barrier, 4 + (z < 7).astype(jnp.int32) + (z > 0).astype(jnp.int32))
+    pl.semaphore_wait(barrier, expected)
 
     def hop(head, kind):
         if kind == 0:
@@ -256,14 +269,22 @@
     docs_copy.start()
 
     sends, takes, ready, owners, count = relay_tables()
-    send_tables = [Table(chip, [sends[c][d] for c in range(BLOCKS)], 10) for d in range(4)]
-    take_tables = [Table(chip, [takes[c][d] for c in range(BLOCKS)], 5) for d in range(4)]
+    links = DIRECTIONS if FAR_ROUNDS else 4
+    send_tables = [Table(chip, [sends[c][d] for c in range(BLOCKS)], 10) for d in range(links)]
+    take_tables = [Table(chip, [takes[c][d] for c in range(BLOCKS)], 5) for d in range(links)]
     ready_table = Table(chip, ready, 3)
     owner_table = Table(chip, owners, 5)
     arrivals = jnp.minimum(chip, WINDOW)
     groups = (arrivals + PER_GROUP - 1) // PER_GROUP
 
     def link_copy(direction, step, head, kind, source, target):
+        if kind is None:
+            return pltpu.make_async_remote_copy(
+                src_ref=kv.at[head, source], dst_ref=kv.at[head, target],
+                send_sem=whole_send.at[direction, step - SPLIT, head],
+                recv_sem=whole_recv.at[direction, step - SPLIT, head],
+                device_id=around[direction], device_id_type=MESH,
+            )
         return pltpu.make_async_remote_copy(
             src_ref=kv.at[head, source, kind], dst_ref=kv.at[head, target, kind],
             send_sem=link_send.at[direction, step, 2 * head + kind],
@@ -272,47 +293,54 @@
         )
 
     def start_round(codes, step, head, kind):
-        for direction in range(4):
-            code = codes[direction]
-
+        for direction, code in enumerate(codes):
             @pl.when(code != 1023)
             def _():
                 link_copy(direction, step, head, kind, code // 32, lax.rem(code, 32)).start()
 
     def take_round(places, step, head, kind):
-        for direction in range(4):
-            place = places[direction]
-
+        for direction, place in enumerate(places):
             @pl.when(place != 31)
             def _():
                 link_copy(direction, step, head, kind, place, place).wait_recv()
 
     def query_copy(index):
-        heads = pl.ds(index * (HEADS // QUERY_COPIES), HEADS // QUERY_COPIES)
+        heads = pl.ds(index * 2, 2)
         return pltpu.make_async_remote_copy(
             src_ref=query_stage.at[heads], dst_ref=queries.at[heads],
             send_sem=query_send.at[index], recv_sem=query_recv.at[index],
             device_id=after, device_id_type=MESH,
         )
 
+    def round_copy(hop_index):
+        last_heads = pl.ds(HEADS - ROUND_HEADS, ROUND_HEADS)
+        return pltpu.make_async_remote_copy(
+            src_ref=query_stage.at[last_heads] if hop_index == 0 else detour.at[hop_index - 1],
+            dst_ref=queries.at[last_heads] if hop_index == 2 else detour.at[hop_index],
+            send_sem=detour_send.at[hop_index], recv_sem=detour_recv.at[hop_index],
+            device_id=before, device_id_type=MESH,
+        )
+
     loads[4].wait()
     loads[5].wait()
 
-    def scale_queries(kv_head):
-        for head in range(kv_head * GROUP, (kv_head + 1) * GROUP):
+    def scale_queries(first_head, last_head):
+        for head in range(first_head, last_head):
             channels = pl.ds(head * HEAD, HEAD)
             query_stage[head] = scaled(q_in[0, :, channels], q_gain, channels)
 
-    scale_queries(0)
-    for index in range(QUERY_COPIES // 2):
+    scale_queries(HEADS - ROUND_HEADS, HEADS)
+    round_copy(0).start()
+    scale_queries(0, GROUP)
+    for index in range(GROUP // 2):
         query_copy(index).start()
     first_codes = [table.at(0) for table in send_tables]
     for head in range(KV_HEADS):
         for kind in range(2):
             hop(head, kind).wait_recv()
             start_round(first_codes, 0, head, kind)
-    scale_queries(1)
-    for index in range(QUERY_COPIES // 2, QUERY_COPIES):
+    scale_queries(GROUP, HEADS - ROUND_HEADS)
+    for index in range(GROUP // 2, QUERY_COPIES):
         query_copy(index).start()
 
     def clear(place, carry):
@@ -397,7 +425,8 @@
                     old = peak[rows].reshape(TILE_ROWS, HEAD)
                     new = jnp.maximum(old, jnp.max(now, axis=1, keepdims=True))
                     shrink = jnp.exp2((old - new) * EXP_SCALE).reshape(shape)
-                weights = jnp.exp2((now - new[:, 0:1]) * EXP_SCALE).astype(jnp.bfloat16)
+                spread = new[:, 0:1] if fresh else jnp.concatenate([new] * (size // HEAD), axis=1)
+                weights = jnp.exp2((now - spread) * EXP_SCALE).astype(jnp.bfloat16)
                 peak[rows] = new.reshape(shape)
                 held[tile] = (weights, shrink)
 
@@ -406,25 +435,50 @@
         at = jnp.minimum(step, ROUNDS - 1)
         later = jnp.minimum(step + 1, ROUNDS - 1)
 
-        @pl.when(step < ROUNDS)
-        def _():
-            places = [table.at(at) for table in take_tables]
+        def exchange(ways, kinds, next_kinds):
+            places = [table.at(at) for table in take_tables[:ways]]
             codes = [
-                jnp.where(step + 1 < ROUNDS, table.at(later), 1023) for table in send_tables
+                jnp.where(step + 1 < ROUNDS, table.at(later), 1023) for table in send_tables[:ways]
             ]
-            for kind in range(2):
+            for kind in kinds:
                 take_round(places, at, stream, kind)
-                start_round(codes, later, stream, kind)
+                if len(next_kinds) == len(kinds):
+                    start_round(codes, later, stream, kind)
+            if len(next_kinds) != len(kinds):
+                start_round(codes, later, stream, None)
+
+        @pl.when(step < SPLIT - 1)
+        def _():
+            exchange(links, (0, 1), (0, 1))
+
+        @pl.when(step == SPLIT - 1)
+        def _():
+            exchange(4, (0, 1), (None,))
+
+        @pl.when((step >= SPLIT) & (step < ROUNDS))
+        def _():
+            exchange(4, (None,), (None,))
+
+        @pl.when(index == FORWARD_STEP)
+        def _():
+            round_copy(0).wait_recv()
+            round_copy(1).start()
+
+        @pl.when(index == FORWARD_STEP_2)
+        def _():
+            round_copy(1).wait_recv()
+            round_copy(2).start()
 
         @pl.when(index == FIRST_STEP)
         def _():
-            for copy in range(QUERY_COPIES // 2):
+            for copy in range(GROUP // 2):
                 query_copy(copy).wait_recv()
 
         @pl.when(index == SECOND_STEP)
         def _():
-            for copy in range(QUERY_COPIES // 2, QUERY_COPIES):
+            for copy in range(GROUP // 2, QUERY_COPIES):
                 query_copy(copy).wait_recv()
+            round_copy(2).wait_recv()
 
         now = jnp.where(step >= ROUNDS, groups, ready_table.at(at))
         past = jnp.where(step == 0, 0, ready_table.at(jnp.maximum(at - 1, 0)))
@@ -457,9 +511,9 @@
     for head in range(HEADS):
         o_ref[0, :, pl.ds(head * HEAD, HEAD)] = (summed[head] / total[head]).astype(jnp.bfloat16)
 
-    def drain(step, carry):
-        for direction in range(4):
-            code = send_tables[direction].at(step)
+    def drain_split(step, carry):
+        for direction, table in enumerate(send_tables):
+            code = table.at(step)
 
             @pl.when(code != 1023)
             def _():
@@ -470,7 +524,20 @@
                         ).wait_send()
         return carry
 
-    lax.fori_loop(0, ROUNDS, drain, 0)
+    def drain_whole(step, carry):
+        for direction, table in enumerate(send_tables[:4]):
+            code = table.at(step)
+
+            @pl.when(code != 1023)
+            def _():
+                for head in range(KV_HEADS):
+                    link_copy(direction, step, head, None, code // 32, lax.rem(code, 32)).wait_send()
+        return carry
+
+    lax.fori_loop(0, SPLIT, drain_split, 0)
+    lax.fori_loop(SPLIT, ROUNDS, drain_whole, 0)
+    for hop_index in range(3):
+        round_copy(hop_index).wait_send()
     for head in range(KV_HEADS):
         hop(head, 0).wait_send()
         hop(head, 1).wait_send()
@@ -482,7 +549,8 @@
 def body(queries, keys, values, modality, query_gain, tower_key_gain, doc_lengths):
     vmem = pl.BlockSpec(memory_space=pltpu.VMEM)
     dma = pltpu.SemaphoreType.DMA
-    return pl.pallas_call(
+    links = DIRECTIONS if FAR_ROUNDS else 4
+    attended = pl.pallas_call(
         kernel,
         out_shape=jax.ShapeDtypeStruct(queries.shape, jnp.bfloat16),
         in_specs=[pl.BlockSpec(memory_space=pltpu.HBM)] * 7,
@@ -505,9 +573,14 @@
             pltpu.VMEM((HEADS, ROWS, HEAD), jnp.float32),
             pltpu.VMEM((HEADS, ROWS, HEAD), jnp.float32),
             pltpu.VMEM((HEADS, ROWS, HEAD), jnp.float32),
+            pltpu.VMEM((2, ROUND_HEADS, ROWS, HEAD), jnp.bfloat16),
             dma((6,)),
-            dma((4, ROUNDS, STREAMS)),
-            dma((4, ROUNDS, STREAMS)),
+            dma((links, SPLIT, STREAMS)),
+            dma((links, SPLIT, STREAMS)),
+            dma((4, ROUNDS - SPLIT, KV_HEADS)),
+            dma((4, ROUNDS - SPLIT, KV_HEADS)),
+            dma((3,)),
+            dma((3,)),
             dma((KV_HEADS, 2)),
             dma((KV_HEADS, 2)),
             dma((QUERY_COPIES,)),
@@ -519,6 +592,7 @@
         ),
         name="relayed_attention",
     )(queries, keys, values, modality, query_gain, tower_key_gain, doc_lengths)
+    return attended
 
 
 def solution(mesh):

time: 62.4 us -> 60.6 us (0.971)
  Pallas kernels: 60.2 us -> 58.3 us
    pallas_call x1, Pallas kernels: 60.2 us -> 58.3 us  [body(): pl.pallas_call(kernel, out_shape=jax.ShapeDtypeStruct(queries.shape, jnp....]
where the time goes in v3:
time: 60.6 us; the launch traced here: 60.4 us
  Pallas kernels  58.3 us (96%)
  local copies, waits for them, and re-layouts  2.09 us (3%)
    pallas_call x1, Pallas kernels, body(): pl.pallas_call(kernel, out_shape=jax.ShapeDtypeStruct(queries.shape, jnp....  58.3 us
    unnamed x1, local copies, waits for them, and re-layouts  2.09 us

profile of v3, /device:TPU:6, one launch (start us, length us, event | category | flops | bytes accessed | tf_op | source)
XLA Modules:
  0.0 60.4 jit_solution(9657131092494672840)
XLA Ops:
  0.0 58.3 %relayed_attention.1 = bf16[1,192,2048]{2,1,0:T(8,128)(2,1)} custom-call(bf16[1,192,2048]{2,1,0:T(8,128)(2,1)} %q_hbm.1, bf16[1,192,256]{2,1,0:T(8,128)(2,1)} %k_hbm.1, bf16[1,192,256]{2,1,0:T(8,128)(2,1)} %v_hbm.1, s32[1,192]{1,0:T(1,128)} %modality_hbm.1, f32[2,2048]{1,0:T(2,128)} %q_gain_hbm.1, f32[2,256]{1,0:T(2,128)} %k_gain_hbm.1, s32[1,16]{1,0:T(1,128)} %docs_hbm.1), custom_call_target="tpu_custom_call" | custom-call | tf_op jit(solution)/shard_map/relayed_attention/pallas_call | solution.py:553
  58.3 2.1 %copy.9 = bf16[1,192,2048]{2,1,0:T(8,128)(2,1)} copy(bf16[1,192,2048]{2,1,0:T(8,128)(2,1)} %relayed_attention.1) | data formatting | bytes 1572864
